TPU v7x, 32 devices: a whole 2x2x4 slice. The times are simulated.
32 devices in a mesh: slab: 2 (over y), gx: 4 (over z), gy: 4 (over x, core).
Axes of the slice: x: 2, y: 2, z: 4, core: 2. Of those that a mesh axis runs over, the one named last changes fastest.
Arguments:
- charge: float32 [32, 512, 512], P(None, ('slab', 'gx'), 'gy'), parts along dimension 1, may hold values from -6 to 6
- surface_charge: float32 [2, 512, 512], P(None, ('slab', 'gx'), 'gy'), parts along dimension 1, may hold values from -6 to 6
Outputs:
- potential: float32 [32, 512, 512], P(None, ('slab', 'gx'), 'gy'), parts along dimension 1
- interface_residual: float32 [32, 512, 512], P(None, ('slab', 'gx'), 'gy'), parts along dimension 1
There are 2 independent parts, one for each index of `slab`. A program takes and returns all parts, laid end to end along the dimension named above; each array names one. Nothing has to cross between parts.
All inputs are finite; a program needn't handle non-finite values.
Results may differ from a plain program's by a relative error of at most 0.0003.
Values sent between devices are 32-bit elements; how exact they have to be, the bound alone decides.
A program may use at most 64 MiB of HBM per device.

v0:
```python
import functools

import jax
import jax.numpy as jnp
import ml_dtypes
import numpy as np
from jax import lax
from jax.experimental import pallas as pl
from jax.experimental.pallas import tpu as pltpu
from jax.sharding import PartitionSpec as P

ITERS = 2


SCREEN = 0.02


def padded(block, sides, width):
    for axis, dim in sides:
        count = lax.axis_size(axis)
        forward = [(i, i + 1) for i in range(count - 1)]
        forward.append((count - 1, 0))
        backward = [(target, source) for source, target in forward]
        low = lax.ppermute(
            lax.slice_in_dim(block, block.shape[dim] - width, None, axis=dim), axis, forward
        )
        high = lax.ppermute(lax.slice_in_dim(block, 0, width, axis=dim), axis, backward)
        block = jnp.concatenate([low, block, high], axis=dim)
    return block


def sine_full(count):
    index = jnp.arange(count).astype(jnp.float32)
    return jnp.sqrt(2.0 / count) * jnp.sin(jnp.pi * jnp.outer(index, index) / count)


def cosine_table(count):
    place = jnp.arange(count).astype(jnp.float32) + 0.5
    order = jnp.arange(count).astype(jnp.float32)
    factor = jnp.where(order == 0.0, jnp.sqrt(1.0 / count), jnp.sqrt(2.0 / count))
    return factor[None, :] * jnp.cos(jnp.pi * jnp.outer(place, order) / count)


def spectrum_table(depth, width, height):
    across = 2.0 - 2.0 * jnp.cos(jnp.pi * jnp.arange(width).astype(jnp.float32) / width)
    along = 2.0 - 2.0 * jnp.cos(jnp.pi * jnp.arange(height).astype(jnp.float32) / height)
    vertical = 2.0 - 2.0 * jnp.cos(jnp.pi * jnp.arange(depth).astype(jnp.float32) / depth)
    return SCREEN + vertical[:, None, None] + across[None, :, None] + along[None, None, :]


def apply_full(field):
    row_rims = jnp.stack([field[:, 0, :], field[:, -1, :]], 1)
    row_ext = padded(row_rims, (("gx", 1),), 1)
    col_rims = jnp.stack([field[:, :, 0], field[:, :, -1]], 0)
    col_ext = padded(col_rims, (("gy", 0),), 1)
    from_below_x = jnp.concatenate([row_ext[:, 0:1, :], field[:, :-1, :]], 1)
    from_above_x = jnp.concatenate([field[:, 1:, :], row_ext[:, 3:4, :]], 1)
    from_below_y = jnp.concatenate([col_ext[0][:, :, None], field[:, :, :-1]], 2)
    from_above_y = jnp.concatenate([field[:, :, 1:], col_ext[3][:, :, None]], 2)
    beside = from_below_x + from_above_x + from_below_y + from_above_y
    upper = jnp.concatenate([field[1:], field[-1:]], 0)
    lower = jnp.concatenate([field[:1], field[:-1]], 0)
    return (6.0 + SCREEN) * field - beside - upper - lower


def solve_interior(field, sines_x, sines_y, cosines, spectrum):
    high = lax.Precision.HIGHEST
    depth, width, height = field.shape
    hat = jnp.dot(field.reshape(depth * width, height), sines_y, precision=high).reshape(
        depth, width, height
    )
    hat = jnp.matmul(sines_x, hat, precision=high)
    hat = jnp.dot(cosines.T, hat.reshape(depth, width * height), precision=high).reshape(
        depth, width, height
    )
    hat = hat / spectrum
    back = jnp.dot(cosines, hat.reshape(depth, width * height), precision=high).reshape(
        depth, width, height
    )
    back = jnp.matmul(sines_x, back, precision=high)
    back = jnp.dot(back.reshape(depth * width, height), sines_y, precision=high)
    return back.reshape(depth, width, height)


def norm_total(residual):
    return lax.psum(jnp.sum(residual * residual), ("gx", "gy"))


def curvature_total(direction, image):
    return lax.psum(jnp.sum(direction * image), ("gx", "gy"))


def on_device(charge, surface_charge):
    depth, width, height = charge.shape
    sines_x = sine_full(width)
    sines_y = sine_full(height)
    cosines = cosine_table(depth)
    spectrum = spectrum_table(depth, width, height)
    row_place = lax.broadcasted_iota(jnp.int32, (1, width, height), 1)
    col_place = lax.broadcasted_iota(jnp.int32, (1, width, height), 2)
    gamma = jnp.where((row_place == 0) | (col_place == 0), 1.0, 0.0).astype(jnp.float32)
    source = charge.at[0].add(surface_charge[0]).at[-1].add(surface_charge[1])
    base = solve_interior(source, sines_x, sines_y, cosines, spectrum)
    reduced = gamma * (source - apply_full(base))
    iterate = jnp.zeros_like(reduced)
    residual = reduced
    direction = reduced
    norm_now = norm_total(residual)
    for step in range(ITERS):
        lifted = -solve_interior(apply_full(direction), sines_x, sines_y, cosines, spectrum)
        image, lifted = (gamma * apply_full(direction + lifted), lifted)
        alpha = norm_now / curvature_total(direction, image)
        iterate = iterate + alpha * direction
        residual = residual - alpha * image
        if step + 1 < ITERS:
            norm_next = norm_total(residual)
            direction = residual + norm_next / norm_now * direction
            norm_now = norm_next
    correction = -solve_interior(apply_full(iterate), sines_x, sines_y, cosines, spectrum)
    potential = iterate + base + correction
    return (potential, residual)


DEPTH, WIDTH, HEIGHT = 32, 64, 128
F32, BF16 = jnp.float32, jnp.bfloat16


def halves(table):
    table = np.asarray(table, np.float64)
    high = table.astype(np.float32).astype(ml_dtypes.bfloat16)
    low = (table - high.astype(np.float64)).astype(np.float32).astype(ml_dtypes.bfloat16)
    return high, low


def sine_unit(count):
    index = np.arange(count)
    table = np.sqrt(2.0 / count) * np.sin(np.pi * np.outer(index, index) / count)
    table[0, 0] = 1.0
    return table


def host_tables():
    place, order = np.arange(DEPTH) + 0.5, np.arange(DEPTH)
    factor = np.where(order == 0, np.sqrt(1.0 / DEPTH), np.sqrt(2.0 / DEPTH))
    cosines = factor[None, :] * np.cos(np.pi * np.outer(place, order) / DEPTH)
    sin_x, sin_y = sine_unit(WIDTH), sine_unit(HEIGHT)
    vertical = 2.0 - 2.0 * np.cos(np.pi * order / DEPTH)
    across = 2.0 - 2.0 * np.cos(np.pi * np.arange(WIDTH) / WIDTH)
    along = 2.0 - 2.0 * np.cos(np.pi * np.arange(HEIGHT) / HEIGHT)
    ux = np.sqrt(2.0 / WIDTH) * np.sin(np.pi * np.arange(WIDTH) / WIDTH)
    uy = np.sqrt(2.0 / HEIGHT) * np.sin(np.pi * np.arange(HEIGHT) / HEIGHT)
    sx = np.where(np.arange(WIDTH) % 2 == 1, 1.0, -1.0)
    sy = np.where(np.arange(HEIGHT) % 2 == 1, 1.0, -1.0)
    sx[0] = sy[0] = 0.0
    ex, ey = np.eye(WIDTH)[0], np.eye(HEIGHT)[0]
    t = {}
    t["zf"] = np.concatenate(halves(np.kron(cosines.T, np.eye(8))))
    t["zi"] = np.concatenate(halves(np.kron(cosines, np.eye(8))))
    t["x"] = np.concatenate(halves(np.kron(np.eye(4), sin_x)))
    y_both = np.concatenate(halves(sin_y), 1)
    t["y"] = np.concatenate([y_both, y_both], 0)
    plane = SCREEN + across[:, None] + along[None, :]
    t["plane"] = plane.astype(np.float32)
    ur = np.concatenate([np.kron(np.eye(4), (ux + ex)[None]), np.kron(np.eye(4), (ux * sx)[None]), np.zeros((8, 4 * WIDTH))], 0)
    t["ur"] = np.concatenate(halves(ur))
    uc = np.zeros((16, HEIGHT))
    uc[0], uc[1], uc[2] = uy + ey, uy * sy, ey
    t["uc"] = np.concatenate(halves(uc))
    spec = plane[None] + vertical[:, None, None]
    inner = np.zeros((WIDTH, HEIGHT))
    inner[1:, 1:] = 1.0
    inv = inner / spec
    t["inv"] = np.where(inner > 0, inv, 1.0).astype(np.float32)
    row_near = np.einsum("a,kab->kb", ux * ux, inv)
    row_far = np.einsum("a,kab->kb", ux * ux * sx, inv)
    col_near = np.einsum("b,kab->ka", uy * uy, inv)
    col_far = np.einsum("b,kab->ka", uy * uy * sy, inv)
    row_coef = SCREEN + vertical[:, None] + 2.0 + along[None, :] - 2.0 * row_near
    col_coef = SCREEN + vertical[:, None] + 2.0 + across[None, :] - 2.0 * col_near
    row_coef[:, 0] = SCREEN + vertical + 4.0
    col_coef[:, 0] = 0.0
    own = np.zeros((DEPTH // 2, 8, HEIGHT))
    own[:, 0], own[:, 1] = row_coef[0::2], row_coef[1::2]
    own[:, 2], own[:, 3] = row_far[0::2], row_far[1::2]
    own[:, 4] = np.concatenate([col_coef[0::2], col_coef[1::2]], 1)
    own[:, 5] = np.concatenate([col_far[0::2], col_far[1::2]], 1)
    own[:, 6], own[:, 7] = vertical[0::2, None], vertical[1::2, None]
    t["own"] = own.astype(np.float32)
    border = np.zeros((WIDTH, HEIGHT))
    border[0], border[:, 0] = uy, ux
    t["pair"] = np.stack([np.outer(ux, uy), border]).astype(np.float32)
    signs = np.zeros((8, HEIGHT))
    signs[0] = sy
    signs[1] = np.concatenate([sx, sx])
    t["signs"] = signs.astype(np.float32)
    zero = np.zeros(WIDTH)
    left = np.zeros((8, HEIGHT))
    left[0], left[1] = np.concatenate([ux + ex, zero]), np.concatenate([zero, ux + ex])
    left[2], left[3] = np.concatenate([ux * sx, zero]), np.concatenate([zero, ux * sx])
    left[6], left[7] = np.concatenate([ex, zero]), np.concatenate([zero, ex])
    right = np.zeros((8, HEIGHT))
    right[4], right[5] = uy + ey, uy * sy
    t["left"], t["right"] = left.astype(np.float32), right.astype(np.float32)
    split = np.concatenate([np.arange(0, DEPTH, 2), np.arange(1, DEPTH, 2)])
    pair_x = np.concatenate(halves(np.kron(np.eye(2), sin_x)), 1)
    wide = np.zeros((DEPTH, 2 * HEIGHT))
    wide[:, :DEPTH] = cosines[split][:, split]
    t["square"] = np.concatenate([pair_x, pair_x] + list(halves(wide)), 0)
    return t


def halved(x):
    high = x.astype(BF16)
    return high, (x - high.astype(F32)).astype(BF16)


def dot(a, b, dims=((1,), (0,))):
    return lax.dot_general(a, b, (dims, ((), ())), preferred_element_type=F32)


def dot_table(table, b, dims=((1,), (0,))):
    count = table.shape[0] // 2
    both = dot(table, b[0], dims)
    return both[:count] + (both[count:] + dot(table[:count], b[1], dims))


def dot_packed(x, table):
    out = dot(jnp.concatenate(halved(x), 1), table)
    half = out.shape[1] // 2
    return out[:, :half] + out[:, half:]


def dot_exact(a, b, dims=((1,), (0,))):
    return lax.dot_general(
        a, b, (dims, ((), ())), precision=lax.Precision.HIGHEST, preferred_element_type=F32
    )


def lane_ids(shape):
    return lax.broadcasted_iota(jnp.int32, shape, len(shape) - 1)


def interior():
    row = lax.broadcasted_iota(jnp.int32, (WIDTH, HEIGHT), 0)
    return (row > 0) & (lane_ids((WIDTH, HEIGHT)) > 0)


def pair_lanes(parts):
    return jnp.concatenate(parts, 1)


def shift_x(n_gx, n_gy, field, by):
    cut = (by % n_gx) * n_gy
    return jnp.concatenate([field[cut:], field[:cut]], 0)


def shift_y(n_gx, n_gy, field, by):
    place = lax.broadcasted_iota(jnp.int32, field.shape, 0) % n_gy
    count = n_gx * n_gy
    ahead = by % count
    plain = jnp.concatenate([field[ahead:], field[:ahead]], 0)
    wrap = (by - n_gy if by > 0 else by + n_gy) % count
    wrapped = jnp.concatenate([field[wrap:], field[:wrap]], 0)
    edge = n_gy - 1 if by > 0 else 0
    return jnp.where(place == edge, wrapped, plain)


def turn_half(x):
    return jnp.concatenate([x[:, WIDTH:], x[:, :WIDTH]], 1)


def schur_modes(n_gx, n_gy, coef, table, row, col):
    row_coef, row_far, col_coef, col_far, row_sign, col_sign = coef
    sx = functools.partial(shift_x, n_gx, n_gy)
    sy = functools.partial(shift_y, n_gx, n_gy)
    count = n_gx * n_gy
    across = jnp.concatenate(halved(jnp.concatenate([col, col * col_sign], 0)), 1)
    across = dot(across, table[0]) + dot(across, table[1])
    along = dot(jnp.concatenate(halved(jnp.concatenate([row, row * row_sign], 0)), 0), table[2])
    along = along[:2 * count] + along[2 * count:]
    along = along[:, :HEIGHT] + along[:, HEIGHT:]
    v = across[:count] + sx(across[count:], -1)
    w = along[:count] + sy(along[count:], -1)
    row_out = row_coef * row - row_far * (sx(row, 1) + sx(row, -1)) - v - row_sign * sy(v, 1)
    col_out = col_coef * col - col_far * (sy(col, 1) + sy(col, -1)) - w - col_sign * sx(w, 1)
    lane = lane_ids((count, HEIGHT))
    row_out = row_out - jnp.concatenate(
        [jnp.where(lane == 0, w, 0.0), jnp.where(lane == 0, turn_half(w), 0.0)], 1
    )
    col_out = jnp.where(
        lane == 0, row_out[:, :HEIGHT], jnp.where(lane == WIDTH, turn_half(row_out[:, HEIGHT:]), col_out)
    )
    return row_out, col_out


def owner_tables(own, pair, turned, signs):
    inner = interior()
    blank = jnp.zeros((WIDTH, HEIGHT), F32)
    lane = lane_ids((HEIGHT, HEIGHT))
    inside = (lane % WIDTH > 0) & (lax.broadcasted_iota(jnp.int32, (HEIGHT, HEIGHT), 0) > 0)
    parts, other = [], []
    for s in range(2):
        vert = own[6 + s:7 + s]
        parts.append(jnp.where(inner, pair[0] / (pair[2] + vert), pair[1]))
        one = jnp.where(inside, turned[0] / (turned[2] + vert), turned[1])
        other.append(jnp.where((lane < WIDTH) == (s == 0), one, 0.0))
    high, low = halved(jnp.concatenate([pair_lanes([parts[0], blank]), pair_lanes([blank, parts[1]])], 0))
    table = (
        jnp.concatenate([high, high], 0),
        jnp.concatenate([low, low], 0),
        jnp.concatenate(halved(jnp.concatenate(other, 0)), 1),
    )
    coef = (
        pair_lanes([own[0:1], own[1:2]]),
        pair_lanes([own[2:3], own[3:4]]),
        own[4:5],
        own[5:6],
        pair_lanes([signs[0:1], signs[0:1]]),
        signs[1:2],
    )
    return coef, table


def start_modes(n_gx, n_gy, fields):
    sx = functools.partial(shift_x, n_gx, n_gy)
    sy = functools.partial(shift_y, n_gx, n_gy)
    row = pair_lanes([fields[0], fields[1]]) + sx(pair_lanes([fields[2], fields[3]]), -1)
    col = fields[4] + sy(fields[5], -1)
    return row, col


def inner_product(first, second):
    lane = lane_ids(first[1].shape)
    cols = jnp.where(lane % WIDTH == 0, 0.0, first[1] * second[1])
    rows = first[0] * second[0]
    down = jnp.sum(rows[:, :HEIGHT] + rows[:, HEIGHT:] + cols, 0, keepdims=True)
    return jnp.sum(down, 1, keepdims=True)


def face_fields(n_gx, n_gy, pair):
    row, col = pair
    beyond = shift_x(n_gx, n_gy, row, 1)
    return [
        row[:, :HEIGHT], row[:, HEIGHT:], beyond[:, :HEIGHT], beyond[:, HEIGHT:],
        col, shift_y(n_gx, n_gy, col, 1),
    ]


def steps(sums):
    rr, rw, ww, wv = sums
    alpha = rr / rw
    after = alpha * alpha * ww - rr
    beta = after / rr
    curve = (1 + beta) * (1 + beta) * rw - 2 * (1 + beta) * alpha * ww + alpha * alpha * wv
    second = after / curve
    return alpha + second * (1 + beta), -second * alpha


def slab_kernel(
    n_gx, n_gy,
    charge_hbm, surface_hbm, z_hbm, x_hbm, y_hbm, ur_hbm, uc_hbm, inv_hbm, own_hbm, pair_hbm, turned_hbm, signs_hbm,
    small_hbm, square_hbm,
    work_hbm, edges_hbm,
    charge, surface, z, x, y, ur, uc, inv, own_ref, pair_ref, turned_ref, signs_ref,
    small, square,
    work, base, edges, faces, msg, got, back, landed, load_sems, store_sems, sems,
):
    count = n_gx * n_gy
    gx, gy = lax.axis_index("gx"), lax.axis_index("gy")
    me = gx * n_gy + gy
    pairs = [(z_hbm, z), (surface_hbm, surface)]
    pairs += [(charge_hbm.at[:, pl.ds(16 * t, 16), :], charge.at[:, pl.ds(16 * t, 16), :]) for t in range(WIDTH // 16)]
    pairs += [(y_hbm, y), (x_hbm, x), (ur_hbm, ur), (uc_hbm, uc)]
    pairs += [(inv_hbm.at[pl.ds(8 * t, 8)], inv.at[pl.ds(8 * t, 8)]) for t in range(DEPTH // 8)]
    pairs += [(own_hbm, own_ref), (pair_hbm, pair_ref), (turned_hbm, turned_ref), (signs_hbm, signs_ref)]
    pairs += [(small_hbm, small), (square_hbm, square)]
    copies = [pltpu.make_async_copy(s, d, load_sems.at[n]) for n, (s, d) in enumerate(pairs)]
    for copy in copies:
        copy.start()

    def partner(off):
        to_x, to_y = gx + off // n_gy, gy + off % n_gy
        to_x = jnp.where(to_x >= n_gx, to_x - n_gx, to_x)
        to_y = jnp.where(to_y >= n_gy, to_y - n_gy, to_y)
        return to_x * n_gy + to_y, {"gx": to_x, "gy": to_y}

    def send(source, target, which, off):
        to, device = partner(off)
        copy = pltpu.make_async_remote_copy(
            src_ref=source.at[to],
            dst_ref=target.at[me],
            send_sem=sems.at[which, 0],
            recv_sem=sems.at[which, 1],
            device_id=device,
            device_id_type=pl.DeviceIdType.MESH,
        )
        copy.start()

    def all_done(buffer, sem):
        whole = buffer.at[pl.ds(0, count - 1)]
        pltpu.make_async_copy(whole, whole, sem).wait()

    barrier = pltpu.get_barrier_semaphore()
    for off in range(1, count):
        pl.semaphore_signal(barrier, inc=1, device_id=partner(off)[1], device_id_type=pl.DeviceIdType.MESH)
    copies[0].wait()
    copies[1].wait()
    ztab = z[...]
    for t in range(WIDTH // 16):
        copies[2 + t].wait()
        sides = []
        for h in range(2):
            at = pl.ds(16 * t + 8 * h, 8)
            block = charge[:, at, :]
            block = jnp.concatenate(
                [block[:1] + surface[0:1, at, :], block[1:-1], block[-1:] + surface[1:2, at, :]], 0
            )
            sides.append(block.reshape(DEPTH * 8, HEIGHT))
        out = dot_table(ztab, halved(pair_lanes(sides)))
        if t == 0:
            copies[6].wait()
            ytab = y[...]
        for h in range(2):
            side = out[:, HEIGHT * h:HEIGHT * (h + 1)]
            side = dot_packed(side, ytab)
            work[:, 16 * t + 8 * h:16 * t + 8 * h + 8, :] = side.reshape(DEPTH, 8, HEIGHT)
    for copy in copies[7:10]:
        copy.wait()
    xtab, utab, ctab = x[...], ur[...], uc[...]
    inner = interior()
    lane = lane_ids((8, HEIGHT))
    pl.semaphore_wait(barrier, count - 1)
    for copy in copies[10:14]:
        copy.wait()
    for step in range(1, n_gx + 1):
        t = partner(n_gy * (step % n_gx))[1]["gx"]
        sides = [work[pl.ds(8 * t + 4 * h, 4)].reshape(4 * WIDTH, HEIGHT) for h in range(2)]
        out = dot_table(xtab, halved(pair_lanes(sides)))
        for h in range(2):
            side = out[:, HEIGHT * h:HEIGHT * (h + 1)].reshape(4, WIDTH, HEIGHT)
            full = []
            corner = []
            for s in range(4):
                k = 8 * t + 4 * h + s
                one = side[s] * inv[k]
                base[k] = jnp.where(inner, one, 0.0)
                full.append(one)
                corner.append(one[0:1])
            full = jnp.concatenate(full, 0)
            parts = halved(full)
            rows = dot_table(utab, parts)
            own = jnp.concatenate(corner + [jnp.zeros((4, HEIGHT), F32)], 0)
            rows = jnp.where(lane == 0, own, rows[:8])
            cols = dot_table(ctab, parts, ((1,), (1,)))
            edge = lane_ids((1, 4 * WIDTH)) % WIDTH == 0
            near = jnp.where(edge, cols[2:3], cols[0:1])
            far = jnp.where(edge, 0.0, cols[1:2])
            for g in range(2):
                at = slice(HEIGHT * g, HEIGHT * (g + 1))
                msg[4 * t + 2 * h + g] = jnp.concatenate(
                    [rows[2 * g:2 * g + 2], rows[4 + 2 * g:6 + 2 * g], near[:, at], far[:, at]],
                    0,
                )
        for ahead in range(1 if step == n_gx else 0, n_gy):
            send(msg, got, 0, n_gy * (step % n_gx) + ahead)
    for copy in copies[14:]:
        copy.wait()
    coef, table = owner_tables(own_ref[me], pair_ref[...], turned_ref[...], signs_ref[...])
    got[me] = msg[me]
    all_done(got, sems.at[0, 1])
    r = start_modes(n_gx, n_gy, [got[:, f, :] for f in range(6)])
    w = schur_modes(n_gx, n_gy, coef, table, *r)
    v = schur_modes(n_gx, n_gy, coef, table, *w)
    for f, field in enumerate(face_fields(n_gx, n_gy, r)):
        back[:, f, :] = field
    for f, field in enumerate(face_fields(n_gx, n_gy, w)):
        back[:, 8 + f, :] = field
    back[:, 6, :] = v[0][:, :HEIGHT]
    back[:, 7, :] = v[0][:, HEIGHT:]
    back[:, 14, :] = v[1]
    sums = (inner_product(r, r), inner_product(r, w), inner_product(w, w), inner_product(w, v))
    lanes = lane_ids((count, HEIGHT))
    back[:, 15, :] = sum(jnp.where(lanes == s, value, 0.0) for s, value in enumerate(sums))
    for off in range(1, count):
        send(back, landed, 1, off)
    landed[me] = back[me]
    all_done(msg, sems.at[0, 0])
    all_done(landed, sems.at[1, 1])
    faces[...] = combine(landed[...])
    stores = inverse(
        faces, base, x, y, inv, small, square, work_hbm, edges_hbm, edges, work, store_sems
    )
    for copy in stores:
        copy.wait()
    all_done(back, sems.at[1, 0])


def combine(landed):
    near, far = landed[:, :8], landed[:, 8:]
    total = jnp.sum(far[:, 7:8, :], 0)
    lane = lane_ids((1, HEIGHT))
    c0, c1 = steps([jnp.sum(jnp.where(lane == s, total, 0.0), 1, keepdims=True) for s in range(4)])
    c0, c1 = c0[None], c1[None]
    lead = near - c0 * far
    rest = [lead[:, 0:2] - c1 * near[:, 6:8], lead[:, 4:5] - c1 * far[:, 6:7], jnp.zeros_like(near[:, :5])]
    return jnp.concatenate([c0 * near + c1 * far] + rest, 1)


def stacked(left, right):
    lh, ll = halved(left)
    rh, rl = halved(right)
    lhs = jnp.concatenate([lh.astype(F32), lh.astype(F32), ll.astype(F32)], 0).astype(BF16)
    rhs = jnp.concatenate([rh.astype(F32), rl.astype(F32), rh.astype(F32)], 0).astype(BF16)
    return dot(lhs, rhs, ((0,), (0,)))


def inverse(
    faces, base, x, y, inv, small, square, work_hbm, edges_hbm, edges, work, store_sems
):
    lane = lane_ids((8, HEIGHT))
    sub = lax.broadcasted_iota(jnp.int32, (8, HEIGHT), 0)
    const_left, const_right = small[0:8], small[8:16]
    xtab, ytab = x[...], y[...]
    half = DEPTH // 2
    rows = dot_packed(jnp.concatenate([faces[:, 8, :], faces[:, 9, :]], 0), ytab)
    cols = dot_packed(faces[:, 10, :], square[0:2 * HEIGHT])
    cols = jnp.concatenate([cols[:, :WIDTH], cols[:, WIDTH:]], 0)
    both = jnp.concatenate([rows, cols, jnp.zeros_like(cols)], 1)
    both = dot_table(square[2 * HEIGHT:, :DEPTH], halved(both))
    rows, cols = both[:, :HEIGHT], both[:, HEIGHT:HEIGHT + WIDTH]
    cols = jnp.concatenate([cols[:half], cols[half:]], 1)
    cols = jnp.where(lane_ids((half, HEIGHT)) % WIDTH == 0, 0.0, cols)
    edges[0:DEPTH] = rows
    edges[DEPTH:] = cols
    for t in range(DEPTH // 8):
        sides = []
        for h in range(2):
            blocks = []
            for g in range(2):
                o = 4 * t + 2 * h + g
                one = faces[o, :8]
                lhs = jnp.where((sub >= 4) & (sub < 6) & (lane % WIDTH > 0), one, const_left)
                up = jnp.concatenate([one[2:], one[:2]], 0)
                rhs = jnp.where((sub < 4) & (lane > 0), one, const_right)
                rhs = jnp.where((sub >= 6) & (lane == 0), up, rhs)
                out = stacked(lhs, rhs)
                for s in range(2):
                    k = 2 * o + s
                    blocks.append(out[WIDTH * s:WIDTH * (s + 1)] * inv[k] + base[k])
            sides.append(jnp.concatenate(blocks, 0))
        out = dot_table(xtab, halved(pair_lanes(sides)))
        for h in range(2):
            side = dot_packed(out[:, HEIGHT * h:HEIGHT * (h + 1)], ytab)
            work[8 * t + 4 * h:8 * t + 4 * h + 4] = side.reshape(4, WIDTH, HEIGHT)
        if t == 0:
            stores = [pltpu.make_async_copy(edges, edges_hbm, store_sems.at[DEPTH // 8])]
            stores[0].start()
        part = pl.ds(8 * t, 8)
        stores.append(pltpu.make_async_copy(work.at[part], work_hbm.at[part], store_sems.at[t]))
        stores[-1].start()
    return stores


def finish_kernel(
    edges_hbm, z_hbm, work_hbm, potential_hbm, residual_hbm,
    edges, z, work, potential, residual, load_sems, store_sems,
):
    pairs = [(edges_hbm, edges), (z_hbm, z)]
    columns = [pl.ds(16 * t, 16) for t in range(WIDTH // 16)]
    pairs += [(work_hbm.at[:, at, :], work.at[:, at, :]) for at in columns]
    loads = [pltpu.make_async_copy(s, d, load_sems.at[n]) for n, (s, d) in enumerate(pairs)]
    for load in loads:
        load.start()
    copies = []
    lane = lane_ids((8, HEIGHT))
    sub = lax.broadcasted_iota(jnp.int32, (8, HEIGHT), 0)
    half = DEPTH // 2
    loads[0].wait()
    unit = jnp.where(lane == 0, 1.0, 0.0)
    mark = jnp.where(((sub == 0) & (lane == 0)) | ((sub == 1) & (lane == WIDTH)), 1.0, 0.0)
    for o in range(half):
        lhs = jnp.where(sub == 2, edges[DEPTH + o:DEPTH + o + 1], mark)
        rhs = jnp.where(sub == 0, edges[o:o + 1], jnp.where(sub == 1, edges[half + o:half + o + 1], jnp.where(sub == 2, unit, 0.0)))
        out = stacked(lhs, rhs)
        residual[2 * o] = out[:WIDTH]
        residual[2 * o + 1] = out[WIDTH:]
        if o % 4 == 3:
            part = pl.ds(2 * (o - 3), 8)
            copies.append(
                pltpu.make_async_copy(residual.at[part], residual_hbm.at[part], store_sems.at[len(copies)])
            )
            copies[-1].start()
    loads[1].wait()
    ztab = z[...]
    for t, at in enumerate(columns):
        loads[2 + t].wait()
        sides = [work[:, 16 * t + 8 * h:16 * t + 8 * h + 8, :].reshape(DEPTH * 8, HEIGHT) for h in range(2)]
        out = dot_table(ztab, halved(pair_lanes(sides)))
        for h in range(2):
            side = out[:, HEIGHT * h:HEIGHT * (h + 1)]
            potential[:, 16 * t + 8 * h:16 * t + 8 * h + 8, :] = side.reshape(DEPTH, 8, HEIGHT)
        copies.append(
            pltpu.make_async_copy(potential.at[:, at, :], potential_hbm.at[:, at, :], store_sems.at[len(copies)])
        )
        copies[-1].start()
    for copy in copies:
        copy.wait()


def on_device_modes(n_gx, n_gy, charge, surface_charge):
    t = host_tables()
    count = n_gx * n_gy
    block = jax.ShapeDtypeStruct(charge.shape, F32)
    hbm = pl.BlockSpec(memory_space=pl.ANY)

    def held(values):
        return [pltpu.VMEM(value.shape, value.dtype) for value in values]

    pair = np.concatenate([t["pair"], t["plane"][None]], 0)
    turned = np.concatenate([np.swapaxes(pair, 1, 2)] * 2, 2)
    args = [charge, surface_charge, t["zf"], t["x"], t["y"], t["ur"], t["uc"], t["inv"], t["own"], pair, turned, t["signs"]]
    six, sixteen = (count, 6, HEIGHT), (count, 16, HEIGHT)
    small = np.concatenate([t["left"], t["right"]], 0)
    args += [small, t["square"]]
    edges = jax.ShapeDtypeStruct((DEPTH + DEPTH // 2, HEIGHT), F32)
    field, rims = pl.pallas_call(
        functools.partial(slab_kernel, n_gx, n_gy),
        out_shape=(block, edges),
        in_specs=[hbm] * len(args),
        out_specs=(hbm, hbm),
        scratch_shapes=held(args)
        + [pltpu.VMEM(shape, F32) for shape in [charge.shape] * 2 + [edges.shape, sixteen, six, six, sixteen, sixteen]]
        + [
            pltpu.SemaphoreType.DMA((20,)),
            pltpu.SemaphoreType.DMA((DEPTH // 8 + 1,)),
            pltpu.SemaphoreType.DMA((2, 2)),
        ],
        compiler_params=pltpu.CompilerParams(collective_id=0, has_side_effects=True),
        name="slab",
    )(*args)
    args = [rims, t["zi"], field]
    return pl.pallas_call(
        finish_kernel,
        out_shape=(block, block),
        in_specs=[hbm] * len(args),
        out_specs=(hbm, hbm),
        scratch_shapes=held(args)
        + [pltpu.VMEM(charge.shape, F32)] * 2
        + [pltpu.SemaphoreType.DMA((2 + WIDTH // 16,)), pltpu.SemaphoreType.DMA((DEPTH // 8 + WIDTH // 16,))],
        name="finish",
    )(*args)


def solution(mesh):
    per_device = functools.partial(on_device_modes, mesh.shape["gx"], mesh.shape["gy"])
    if (mesh.shape["gx"], mesh.shape["gy"]) != (4, 4):
        per_device = on_device
    in_specs = (P(None, ("slab", "gx"), "gy"), P(None, ("slab", "gx"), "gy"))
    out_specs = (P(None, ("slab", "gx"), "gy"), P(None, ("slab", "gx"), "gy"))
    return jax.shard_map(
        per_device, mesh=mesh, in_specs=in_specs, out_specs=out_specs, check_vma=False
    )
```

profile of v0, /device:TPU:0, one launch (start us, length us, event | category | flops | bytes accessed | tf_op | source)
XLA Modules:
  0.0 25.0 jit_solution(3620750328871289278)
XLA Ops:
  0.6 21.0 %slab.1 = (f32[32,64,128]{2,1,0:T(8,128)}, f32[48,128]{1,0:T(8,128)}) custom-call(f32[32,64,128]{2,1,0:T(8,128)} %charge_hbm.1, f32[2,64,128]{2,1,0:T(8,128)} %surface_hbm.1, bf16[512,256]{1,0:T(8,128)(2,1)} %constant.26.clone.z_hbm, bf16[512,256]{1,0:T(8,128)(2,1)} %constant.27.clone.x_hbm, bf16[256,256]{1,0:T(8,128)(2,1)} %constant.28.clone.y_hbm, ...), custom_call_target="tpu_custom_call" | custom-call | tf_op jit(solution)/shard_map/slab/pallas_call | solution.py:626
  21.6 3.4 %finish.1 = (f32[32,64,128]{2,1,0:T(8,128)}, f32[32,64,128]{2,1,0:T(8,128)}) custom-call(f32[48,128]{1,0:T(8,128)} %get-tuple-element.4.edges_hbm, bf16[512,256]{1,0:T(8,128)(2,1)} %constant.38.clone.z_hbm, f32[32,64,128]{2,1,0:T(8,128)} %get-tuple-element.5.work_hbm), custom_call_target="tpu_custom_call" | custom-call | tf_op jit(solution)/shard_map/finish/pallas_call | solution.py:642
where the time goes:
time: 25.1 us; the launch traced here: 25 us
  Pallas kernels  24.3 us (97%)
  between operations  0.64 us (3%)
    pallas_call x1, Pallas kernels, on_device_modes(): pl.pallas_call(functools.partial(slab_kernel, n_gx, n_gy), out_shape=(blo...  21 us
    pallas_call x1, Pallas kernels, on_device_modes(): pl.pallas_call(finish_kernel, out_shape=(block, block), in_specs=[hbm] *...  3.36 us

commit v1 on v0

--- a/solution.py
+++ b/solution.py
@@ -432,7 +432,8 @@
     pl.semaphore_wait(barrier, count - 1)
     for copy in copies[10:14]:
         copy.wait()
-    for step in range(1, n_gx + 1):
+    far_first = sorted(range(n_gx), key=lambda d: -min(d, n_gx - d))
+    for step in far_first:
         t = partner(n_gy * (step % n_gx))[1]["gx"]
         sides = [work[pl.ds(8 * t + 4 * h, 4)].reshape(4 * WIDTH, HEIGHT) for h in range(2)]
         out = dot_table(xtab, halved(pair_lanes(sides)))
@@ -461,7 +462,7 @@
                     [rows[2 * g:2 * g + 2], rows[4 + 2 * g:6 + 2 * g], near[:, at], far[:, at]],
                     0,
                 )
-        for ahead in range(1 if step == n_gx else 0, n_gy):
+        for ahead in range(1 if step == 0 else 0, n_gy):
             send(msg, got, 0, n_gy * (step % n_gx) + ahead)
     for copy in copies[14:]:
         copy.wait()
@@ -481,8 +482,9 @@
     sums = (inner_product(r, r), inner_product(r, w), inner_product(w, w), inner_product(w, v))
     lanes = lane_ids((count, HEIGHT))
     back[:, 15, :] = sum(jnp.where(lanes == s, value, 0.0) for s, value in enumerate(sums))
-    for off in range(1, count):
-        send(back, landed, 1, off)
+    for step in far_first:
+        for ahead in range(1 if step == 0 else 0, n_gy):
+            send(back, landed, 1, n_gy * step + ahead)
     landed[me] = back[me]
     all_done(msg, sems.at[0, 0])
     all_done(landed, sems.at[1, 1])

time: 25.1 us -> 25.7 us (1.024)
  Pallas kernels: 24.3 us -> 24.9 us
    pallas_call x1, Pallas kernels: 21 us -> 21.6 us  [on_device_modes(): pl.pallas_call(functools.partial(slab_kernel, n_gx, n_gy), out_shape=(blo...]
where the time goes in v1:
time: 25.7 us; the launch traced here: 25.6 us
  Pallas kernels  24.9 us (97%)
  between operations  0.64 us (2%)
    pallas_call x1, Pallas kernels, on_device_modes(): pl.pallas_call(functools.partial(slab_kernel, n_gx, n_gy), out_shape=(blo...  21.6 us
    pallas_call x1, Pallas kernels, on_device_modes(): pl.pallas_call(finish_kernel, out_shape=(block, block), in_specs=[hbm] *...  3.36 us

profile of v1, /device:TPU:0, one launch (start us, length us, event | category | flops | bytes accessed | tf_op | source)
XLA Modules:
  0.0 25.6 jit_solution(13733025391236441917)
XLA Ops:
  0.6 21.6 %slab.1 = (f32[32,64,128]{2,1,0:T(8,128)}, f32[48,128]{1,0:T(8,128)}) custom-call(f32[32,64,128]{2,1,0:T(8,128)} %charge_hbm.1, f32[2,64,128]{2,1,0:T(8,128)} %surface_hbm.1, bf16[512,256]{1,0:T(8,128)(2,1)} %constant.26.clone.z_hbm, bf16[512,256]{1,0:T(8,128)(2,1)} %constant.27.clone.x_hbm, bf16[256,256]{1,0:T(8,128)(2,1)} %constant.28.clone.y_hbm, ...), custom_call_target="tpu_custom_call" | custom-call | tf_op jit(solution)/shard_map/slab/pallas_call | solution.py:628
  22.2 3.4 %finish.1 = (f32[32,64,128]{2,1,0:T(8,128)}, f32[32,64,128]{2,1,0:T(8,128)}) custom-call(f32[48,128]{1,0:T(8,128)} %get-tuple-element.4.edges_hbm, bf16[512,256]{1,0:T(8,128)(2,1)} %constant.38.clone.z_hbm, f32[32,64,128]{2,1,0:T(8,128)} %get-tuple-element.5.work_hbm), custom_call_target="tpu_custom_call" | custom-call | tf_op jit(solution)/shard_map/finish/pallas_call | solution.py:644
